TPU v7x, 32 devices: a whole 2x2x4 slice. The times are simulated.
32 devices in a mesh: section: 2 (over core), tensor: 2 (over x), dp: 8 (over z, y).
Axes of the slice: x: 2, y: 2, z: 4, core: 2. Of those that a mesh axis runs over, the one named last changes fastest.
Arguments:
- inputs: bfloat16 [16, 1024, 768], P('dp', 'tensor'), may hold values from -6 to 6
- segments: int32 [16, 1024], P('dp'), may hold values from 0 to 3, never falling along the last dimension, each value on 1 to 768 neighbouring positions
- cotangent: bfloat16 [16, 1024, 768], P('dp', 'tensor'), may hold values from -6 to 6
- norm_gains: bfloat16 [2, 2, 768], P('section'), may hold values from 0.5 to 1.5
- shared_biases: bfloat16 [2, 4, 768], P('section'), may hold values from -1.5 to 1.5
- w_qkv: bfloat16 [2, 768, 3, 768], P('section', None, None, 'tensor'), may hold values from -0.3125 to 0.3125
- qv_bias: bfloat16 [2, 2, 768], P('section', None, 'tensor'), may hold values from -1.5 to 1.5
- w_out: bfloat16 [2, 768, 768], P('section', 'tensor'), may hold values from -0.875 to 0.875
- w_up: bfloat16 [2, 768, 3072], P('section', None, 'tensor'), may hold values from -0.21875 to 0.21875
- up_bias: bfloat16 [2, 3072], P('section', 'tensor'), may hold values from -1.5 to 1.5
- w_down: bfloat16 [2, 3072, 768], P('section', 'tensor'), may hold values from -0.109375 to 0.109375
Outputs:
- activations: bfloat16 [2, 16, 1024, 768], P('section', 'dp', 'tensor')
- input_grads: bfloat16 [2, 16, 1024, 768], P('section', 'dp', 'tensor')
- grad_qkv: float32 [2, 768, 3, 768], P('section', None, None, 'tensor')
- grad_qv_bias: float32 [2, 2, 768], P('section', None, 'tensor')
- grad_out: float32 [2, 768, 768], P('section', 'tensor')
- grad_up: float32 [2, 768, 3072], P('section', None, 'tensor')
- grad_up_bias: float32 [2, 3072], P('section', 'tensor')
- grad_down: float32 [2, 3072, 768], P('section', 'tensor')
- grad_gains: float32 [2, 2, 768], P('section')
- grad_shifts: float32 [2, 4, 768], P('section')
Inputs may be any that keep to these rules, and one draw needn't show every extreme that they name: `segments`: each row's numbers never fall; a number's run is 1 to 768 tokens long, and one run of every row has exactly that length.
All inputs are finite; a program needn't handle non-finite values.
Results may differ from a plain program's by a relative error of at most 0.03.
Values may be sent and summed in bfloat16 or wider, within the bound.
A program may use at most 320 MiB of HBM per device.

v0:
```python
import jax
import jax.numpy as jnp
from jax import lax
from jax.sharding import PartitionSpec as P

HEAD = 64
eps_norm = 1e-05


def shifted(block, axis, distance):
    devices = range(lax.axis_size(axis))
    route = [(i - distance, i) for i in devices if i - distance in devices]
    return lax.ppermute(block, axis, route)


def smooth(values_in):
    return jax.nn.gelu(values_in, approximate=True)


def dot_rows(left, right):
    return lax.dot_general(
        left, right, (((0,), (0,)), ((), ())), preferred_element_type=jnp.float32
    )


def dot_last(left, right):
    return lax.dot_general(
        left, right, (((1,), (1,)), ((), ())), preferred_element_type=jnp.float32
    )


def norm_forward(rows_in, gain, shift):
    row_mean = jnp.mean(rows_in, axis=-1, keepdims=True)
    centred = rows_in - row_mean
    inv_dev = lax.rsqrt(jnp.mean(centred * centred, axis=-1, keepdims=True) + eps_norm)
    unit_rows = centred * inv_dev
    return (unit_rows * gain + shift, unit_rows, inv_dev)


def norm_backward(grad_out, unit_rows, inv_dev, gain):
    scaled = grad_out * gain
    grad_in = inv_dev * (
        scaled
        - jnp.mean(scaled, axis=-1, keepdims=True)
        - unit_rows * jnp.mean(scaled * unit_rows, axis=-1, keepdims=True)
    )
    return (grad_in, jnp.sum(grad_out * unit_rows, axis=0), jnp.sum(grad_out, axis=0))


def block_shape(seq_total):
    block_count = max(1, seq_total // 512)
    return (block_count, seq_total // block_count)


def allowed_block(begin_at, block_len, seg_ids):
    q_pos = begin_at + jnp.arange(block_len)
    k_pos = jnp.arange(seg_ids.shape[0])
    q_seg = seg_ids[begin_at : begin_at + block_len]
    return (k_pos[None, :] <= q_pos[:, None]) & (q_seg[:, None] == seg_ids[None, :])


def attention_forward(queries, key_rows, value_rows, seg_ids):
    block_count, block_len = block_shape(queries.shape[0])
    pieces, totals = ([], [])
    for block_no in range(block_count):
        begin_at = block_no * block_len
        scores = jnp.einsum(
            "qhd,khd->hqk",
            queries[begin_at : begin_at + block_len],
            key_rows,
            preferred_element_type=jnp.float32,
        )
        scores = jnp.where(allowed_block(begin_at, block_len, seg_ids)[None], scores, -1e30)
        row_top = jnp.max(scores, axis=-1, keepdims=True)
        weights = jnp.exp(scores - row_top)
        summed = jnp.sum(weights, axis=-1, keepdims=True)
        prob_rows = (weights / summed).astype(jnp.bfloat16)
        pieces.append(
            jnp.einsum("hqk,khd->qhd", prob_rows, value_rows, preferred_element_type=jnp.float32)
        )
        totals.append(row_top + jnp.log(summed))
    return (jnp.concatenate(pieces, axis=0), jnp.concatenate(totals, axis=1))


def attention_backward(queries, key_rows, value_rows, seg_ids, totals, grad_mixed):
    block_count, block_len = block_shape(queries.shape[0])
    grad_queries = []
    grad_keys = jnp.zeros(key_rows.shape, jnp.float32)
    grad_values = jnp.zeros(value_rows.shape, jnp.float32)
    for block_no in range(block_count):
        begin_at = block_no * block_len
        part_query = queries[begin_at : begin_at + block_len]
        part_grad = grad_mixed[begin_at : begin_at + block_len]
        scores = jnp.einsum(
            "qhd,khd->hqk", part_query, key_rows, preferred_element_type=jnp.float32
        )
        scores = jnp.where(allowed_block(begin_at, block_len, seg_ids)[None], scores, -1e30)
        prob_exact = jnp.exp(scores - totals[:, begin_at : begin_at + block_len])
        prob_rows = prob_exact.astype(jnp.bfloat16)
        grad_probs = jnp.einsum(
            "qhd,khd->hqk", part_grad, value_rows, preferred_element_type=jnp.float32
        )
        row_dot = jnp.sum(prob_exact * grad_probs, axis=-1, keepdims=True)
        grad_scores = (prob_exact * (grad_probs - row_dot)).astype(jnp.bfloat16)
        grad_queries.append(
            jnp.einsum("hqk,khd->qhd", grad_scores, key_rows, preferred_element_type=jnp.float32)
        )
        grad_keys = grad_keys + jnp.einsum(
            "hqk,qhd->khd", grad_scores, part_query, preferred_element_type=jnp.float32
        )
        grad_values = grad_values + jnp.einsum(
            "hqk,qhd->khd", prob_rows, part_grad, preferred_element_type=jnp.float32
        )
    return (jnp.concatenate(grad_queries, axis=0), grad_keys, grad_values)


def local(
    inputs,
    segments,
    cotangent,
    norm_gains,
    shared_biases,
    w_qkv,
    qv_bias,
    w_out,
    w_up,
    up_bias,
    w_down,
):
    is_first = lax.axis_index("section") == 0
    micro_count, half_rows, model_width = inputs.shape
    local_width = w_qkv.shape[3]
    head_count = local_width // HEAD
    q_scale = HEAD ** (-0.5)
    gain_rows = norm_gains[0].astype(jnp.float32)
    shifts = shared_biases[0].astype(jnp.float32)
    qkv_mat = w_qkv[0].reshape(model_width, 3 * local_width)
    qv_rows = qv_bias[0].astype(jnp.float32)
    out_mat = w_out[0]
    up_mat, down_mat, up_vec = (w_up[0], w_down[0], up_bias[0])
    up_shift = up_vec.astype(jnp.float32)
    zero_rows = jnp.zeros((half_rows, model_width), jnp.bfloat16)
    received = zero_rows
    outputs, kept_all = ([], [])
    for tick_no in range(micro_count + 1):
        own_micro = min(tick_no, micro_count - 1)
        prior_micro = max(tick_no - 1, 0)
        layer_in = jnp.where(is_first, inputs[own_micro], received).astype(jnp.float32)
        seg_ids = jnp.where(is_first, segments[own_micro], segments[prior_micro])
        normed, forward_unit1, forward_inv1 = norm_forward(layer_in, gain_rows[0], shifts[0])
        forward_normed_all = lax.all_gather(
            normed.astype(jnp.bfloat16), "tensor", axis=0, tiled=True
        )
        forward_seq_total = forward_normed_all.shape[0]
        projected = jnp.dot(
            forward_normed_all, qkv_mat, preferred_element_type=jnp.float32
        ).reshape(forward_seq_total, 3, local_width)
        forward_queries = (
            ((projected[:, 0] + qv_rows[0]) * q_scale)
            .astype(jnp.bfloat16)
            .reshape(forward_seq_total, head_count, HEAD)
        )
        forward_key_rows = (
            projected[:, 1].astype(jnp.bfloat16).reshape(forward_seq_total, head_count, HEAD)
        )
        forward_value_rows = (
            (projected[:, 2] + qv_rows[1])
            .astype(jnp.bfloat16)
            .reshape(forward_seq_total, head_count, HEAD)
        )
        forward_mixed_rows, forward_totals = attention_forward(
            forward_queries, forward_key_rows, forward_value_rows, seg_ids
        )
        forward_mixed_rows = forward_mixed_rows.reshape(forward_seq_total, local_width).astype(
            jnp.bfloat16
        )
        middle = (
            layer_in
            + lax.psum_scatter(
                jnp.dot(forward_mixed_rows, out_mat, preferred_element_type=jnp.float32).astype(
                    jnp.bfloat16
                ),
                "tensor",
                scatter_dimension=0,
                tiled=True,
            ).astype(jnp.float32)
            + shifts[2]
        )
        forward_normed2, forward_unit2, forward_inv2 = norm_forward(middle, gain_rows[1], shifts[1])
        forward_normed2 = forward_normed2.astype(jnp.bfloat16)
        forward_normed2 = lax.all_gather(forward_normed2, "tensor", axis=0, tiled=True)
        forward_hidden = (
            jnp.dot(forward_normed2, up_mat, preferred_element_type=jnp.float32) + up_shift
        )
        forward_active = smooth(forward_hidden).astype(jnp.bfloat16)
        branch2 = lax.psum_scatter(
            jnp.dot(forward_active, down_mat, preferred_element_type=jnp.float32).astype(
                jnp.bfloat16
            ),
            "tensor",
            scatter_dimension=0,
            tiled=True,
        ).astype(jnp.float32)
        output = (middle + branch2 + shifts[3]).astype(jnp.bfloat16)
        forward_kept_state = (
            seg_ids,
            forward_unit1,
            forward_inv1,
            forward_normed_all,
            forward_queries,
            forward_key_rows,
            forward_value_rows,
            forward_totals,
            forward_mixed_rows,
            forward_unit2,
            forward_inv2,
            forward_normed2,
            forward_hidden,
            forward_active,
        )
        output, kept_state = (output, forward_kept_state)
        outputs.append(output)
        kept_all.append(kept_state)
        if tick_no < micro_count:
            received = shifted(output, "section", 1)
    grad_sums = (
        jnp.zeros((model_width, 3 * local_width), jnp.float32),
        jnp.zeros((2, local_width), jnp.float32),
        jnp.zeros(out_mat.shape, jnp.float32),
        jnp.zeros(up_mat.shape, jnp.float32),
        jnp.zeros(up_vec.shape, jnp.float32),
        jnp.zeros(down_mat.shape, jnp.float32),
        jnp.zeros((2, model_width), jnp.float32),
        jnp.zeros((4, model_width), jnp.float32),
    )
    received = zero_rows
    grads_in = []
    for tick_no in range(micro_count + 1):
        kept_slot = micro_count - tick_no
        fresh_grad = cotangent[kept_slot - 1] if kept_slot >= 1 else zero_rows
        incoming = jnp.where(is_first, received, fresh_grad).astype(jnp.float32)
        (
            backward_seg_ids,
            unit1,
            inv1,
            normed_all,
            queries,
            key_rows,
            value_rows,
            totals,
            mixed_rows,
            unit2,
            inv2,
            normed2,
            hidden,
            active,
        ) = kept_all[kept_slot]
        (
            backward_g_qkv,
            backward_g_qv,
            backward_g_out,
            backward_g_up,
            backward_g_upb,
            backward_g_down,
            backward_g_gain,
            backward_g_shift,
        ) = grad_sums
        seq_total = normed_all.shape[0]
        grad_branch2 = incoming.astype(jnp.bfloat16)
        ignored, gelu_back = jax.vjp(smooth, hidden)
        grad_all = lax.all_gather(grad_branch2, "tensor", axis=0, tiled=True)
        grad_active = dot_last(grad_all, down_mat)
        backward_g_down = backward_g_down + dot_rows(active, grad_all)
        grad_hidden = gelu_back(grad_active)[0].astype(jnp.bfloat16)
        backward_g_up = backward_g_up + dot_rows(normed2, grad_hidden)
        backward_g_upb = backward_g_upb + jnp.sum(grad_hidden.astype(jnp.float32), axis=0)
        grad_normed2 = lax.psum_scatter(
            dot_last(grad_hidden, up_mat).astype(jnp.bfloat16),
            "tensor",
            scatter_dimension=0,
            tiled=True,
        ).astype(jnp.float32)
        norm2_grad, gain2, shift2 = norm_backward(grad_normed2, unit2, inv2, gain_rows[1])
        grad_middle = incoming + norm2_grad
        grad_branch = grad_middle.astype(jnp.bfloat16)
        grad_branch_all = lax.all_gather(grad_branch, "tensor", axis=0, tiled=True)
        backward_g_out = backward_g_out + dot_rows(mixed_rows, grad_branch_all)
        grad_mixed = (
            dot_last(grad_branch_all, out_mat)
            .astype(jnp.bfloat16)
            .reshape(seq_total, head_count, HEAD)
        )
        grad_queries, grad_keys, grad_values = attention_backward(
            queries, key_rows, value_rows, backward_seg_ids, totals, grad_mixed
        )
        grad_queries = (grad_queries * q_scale).astype(jnp.bfloat16).reshape(seq_total, local_width)
        grad_keys = grad_keys.astype(jnp.bfloat16).reshape(seq_total, local_width)
        grad_values = grad_values.astype(jnp.bfloat16).reshape(seq_total, local_width)
        grad_proj = jnp.concatenate([grad_queries, grad_keys, grad_values], axis=1)
        backward_g_qkv = backward_g_qkv + dot_rows(normed_all, grad_proj)
        backward_g_qv = backward_g_qv + jnp.stack(
            [
                jnp.sum(grad_queries.astype(jnp.float32), axis=0),
                jnp.sum(grad_values.astype(jnp.float32), axis=0),
            ]
        )
        grad_normed = lax.psum_scatter(
            dot_last(grad_proj, qkv_mat).astype(jnp.bfloat16),
            "tensor",
            scatter_dimension=0,
            tiled=True,
        ).astype(jnp.float32)
        norm1_grad, gain1, shift1 = norm_backward(grad_normed, unit1, inv1, gain_rows[0])
        grad_in = grad_middle + norm1_grad
        backward_g_gain = backward_g_gain + jnp.stack([gain1, gain2])
        backward_g_shift = backward_g_shift + jnp.stack(
            [
                shift1,
                shift2,
                jnp.sum(grad_branch.astype(jnp.float32), axis=0),
                jnp.sum(grad_branch2.astype(jnp.float32), axis=0),
            ]
        )
        grad_in, grad_sums = (
            grad_in.astype(jnp.bfloat16),
            (
                backward_g_qkv,
                backward_g_qv,
                backward_g_out,
                backward_g_up,
                backward_g_upb,
                backward_g_down,
                backward_g_gain,
                backward_g_shift,
            ),
        )
        grads_in.append(grad_in)
        if tick_no < micro_count:
            received = shifted(grad_in, "section", -1)
    act_rows = jnp.stack(
        [
            jnp.where(is_first, outputs[index_no], outputs[index_no + 1])
            for index_no in range(micro_count)
        ]
    )
    grad_rows_out = jnp.stack(
        [
            jnp.where(
                is_first, grads_in[micro_count - index_no], grads_in[micro_count - 1 - index_no]
            )
            for index_no in range(micro_count)
        ]
    )
    g_qkv, g_qv, g_out, g_up, g_upb, g_down, g_gain, g_shift = grad_sums
    g_qkv, g_qv, g_out, g_up, g_upb, g_down = lax.psum(
        (g_qkv, g_qv, g_out, g_up, g_upb, g_down), "dp"
    )
    g_gain, g_shift = lax.psum((g_gain, g_shift), ("tensor", "dp"))
    return (
        act_rows[None],
        grad_rows_out[None],
        g_qkv.reshape(model_width, 3, local_width)[None],
        g_qv[None],
        g_out[None],
        g_up[None],
        g_upb[None],
        g_down[None],
        g_gain[None],
        g_shift[None],
    )


def solution(mesh):
    return jax.shard_map(
        local,
        mesh=mesh,
        in_specs=(
            P("dp", "tensor", None),
            P("dp", None),
            P("dp", "tensor", None),
            P("section", None, None),
            P("section", None, None),
            P("section", None, None, "tensor"),
            P("section", None, "tensor"),
            P("section", "tensor", None),
            P("section", None, "tensor"),
            P("section", "tensor"),
            P("section", "tensor", None),
        ),
        out_specs=(
            P("section", "dp", "tensor", None),
            P("section", "dp", "tensor", None),
            P("section", None, None, "tensor"),
            P("section", None, "tensor"),
            P("section", "tensor", None),
            P("section", None, "tensor"),
            P("section", "tensor"),
            P("section", "tensor", None),
            P("section", None, None),
            P("section", None, None),
        ),
        check_vma=False,
    )
```

profile of v0, /device:TPU:0, one launch (start us, length us, event | category | flops | bytes accessed | tf_op | source)
XLA Modules:
  0.0 1564.0 jit_solution(2588667289465846196)
XLA Ops:
  20.0 24.2 %all-gather.14.cloned.1.call-done = bf16[1024,768]{1,0:T(8,128)(2,1)} async-done(((bf16[512,768]{1,0:T(8,128)(2,1)}), bf16[1024,768]{1,0:T(8,128)(2,1)}) %all-gather.14.cloned.1.call-update) | async-done | bytes 1572880 | tf_op jit(solution)/shard_map/all_gather | solution.py:151
  59.2 4.1 fusion.233
  70.1 4.1 fusion.234
  76.7 26.0 %reduce-scatter.13.cloned.1.call-done = bf16[512,768]{1,0:T(8,128)(2,1)} async-done(((bf16[1024,768]{1,0:T(8,128)(2,1)}), bf16[512,768]{1,0:T(8,128)(2,1)}) %reduce-scatter.13.cloned.1.call-update) | async-done | bytes 786448 | tf_op jit(solution)/shard_map/reduce_scatter | solution.py:179
  108.1 27.3 %all-gather.16.cloned.1.call-done = bf16[1024,768]{1,0:T(8,128)(2,1)} async-done(((bf16[512,768]{1,0:T(8,128)(2,1)}), bf16[1024,768]{1,0:T(8,128)(2,1)}) %all-gather.16.cloned.1.call-update) | async-done | bytes 1572880 | tf_op jit(solution)/shard_map/all_gather | solution.py:191
  135.4 4.1 fusion.97
  142.1 5.0 fusion.152
  147.2 26.2 %reduce-scatter.15.cloned.1.call-done = bf16[512,768]{1,0:T(8,128)(2,1)} async-done(((bf16[1024,768]{1,0:T(8,128)(2,1)}), bf16[512,768]{1,0:T(8,128)(2,1)}) %reduce-scatter.15.cloned.1.call-update) | async-done | bytes 786448 | tf_op jit(solution)/shard_map/reduce_scatter | solution.py:196
  182.9 25.4 %all-gather.18.cloned.1.call-done = bf16[1024,768]{1,0:T(8,128)(2,1)} async-done(((bf16[512,768]{1,0:T(8,128)(2,1)}), bf16[1024,768]{1,0:T(8,128)(2,1)}) %all-gather.18.cloned.1.call-update) | async-done | bytes 1572880 | tf_op jit(solution)/shard_map/all_gather | solution.py:151
  220.6 4.1 fusion.231
  231.5 4.1 fusion.232
  239.0 25.8 %reduce-scatter.17.cloned.1.call-done = bf16[512,768]{1,0:T(8,128)(2,1)} async-done(((bf16[1024,768]{1,0:T(8,128)(2,1)}), bf16[512,768]{1,0:T(8,128)(2,1)}) %reduce-scatter.17.cloned.1.call-update) | async-done | bytes 786448 | tf_op jit(solution)/shard_map/reduce_scatter | solution.py:179
  269.4 27.3 %all-gather.20.cloned.1.call-done = bf16[1024,768]{1,0:T(8,128)(2,1)} async-done(((bf16[512,768]{1,0:T(8,128)(2,1)}), bf16[1024,768]{1,0:T(8,128)(2,1)}) %all-gather.20.cloned.1.call-update) | async-done | bytes 1572880 | tf_op jit(solution)/shard_map/all_gather | solution.py:191
  296.8 6.9 multiply_convert_fusion.7
  309.0 26.2 %reduce-scatter.19.cloned.1.call-done = bf16[512,768]{1,0:T(8,128)(2,1)} async-done(((bf16[1024,768]{1,0:T(8,128)(2,1)}), bf16[512,768]{1,0:T(8,128)(2,1)}) %reduce-scatter.19.cloned.1.call-update) | async-done | bytes 786448 | tf_op jit(solution)/shard_map/reduce_scatter | solution.py:196
  345.9 25.4 %all-gather.22.cloned.1.call-done = bf16[1024,768]{1,0:T(8,128)(2,1)} async-done(((bf16[512,768]{1,0:T(8,128)(2,1)}), bf16[1024,768]{1,0:T(8,128)(2,1)}) %all-gather.22.cloned.1.call-update) | async-done | bytes 1572880 | tf_op jit(solution)/shard_map/all_gather | solution.py:151
  384.1 4.1 fusion.230
  395.0 4.1 fusion.229
  402.3 26.0 %reduce-scatter.21.cloned.1.call-done = bf16[512,768]{1,0:T(8,128)(2,1)} async-done(((bf16[1024,768]{1,0:T(8,128)(2,1)}), bf16[512,768]{1,0:T(8,128)(2,1)}) %reduce-scatter.21.cloned.1.call-update) | async-done | bytes 786448 | tf_op jit(solution)/shard_map/reduce_scatter | solution.py:179
  436.3 24.5 %all-gather.24.cloned.1.call-done = bf16[1024,768]{1,0:T(8,128)(2,1)} async-done(((bf16[512,768]{1,0:T(8,128)(2,1)}), bf16[1024,768]{1,0:T(8,128)(2,1)}) %all-gather.24.cloned.1.call-update) | async-done | bytes 1572880 | tf_op jit(solution)/shard_map/all_gather | solution.py:191
  460.8 5.9 fusion.93
  466.7 23.4 %all-gather.36.cloned.1.call-done = bf16[1,1024,768]{2,1,0:T(8,128)(2,1)} async-done(((bf16[1,512,768]{2,1,0:T(8,128)(2,1)}), bf16[1,1024,768]{2,1,0:T(8,128)(2,1)}) %all-gather.36.cloned.1.call-update) | async-done | bytes 1572880 | tf_op jit(solution)/shard_map/all_gather | solution.py:271
  490.1 9.4 convert_reduce_fusion.2
  505.0 26.2 %reduce-scatter.25.cloned.1.call-done = bf16[512,768]{1,0:T(8,128)(2,1)} async-done(((bf16[1024,768]{1,0:T(8,128)(2,1)}), bf16[512,768]{1,0:T(8,128)(2,1)}) %reduce-scatter.25.cloned.1.call-update) | async-done | bytes 786448 | tf_op jit(solution)/shard_map/reduce_scatter | solution.py:277
  540.6 24.6 %all-gather.26.cloned.1.call-done = bf16[1024,768]{1,0:T(8,128)(2,1)} async-done(((bf16[512,768]{1,0:T(8,128)(2,1)}), bf16[1024,768]{1,0:T(8,128)(2,1)}) %all-gather.26.cloned.1.call-update) | async-done | bytes 1572880 | tf_op jit(solution)/shard_map/all_gather | solution.py:286
  568.5 11.5 multiply_reduce_fusion.5
  581.2 6.7 multiply_convert_fusion.5
  592.2 6.3 fusion.20
  598.5 9.6 multiply_reduce_fusion.4
  611.8 10.1 multiply_convert_fusion.4
  630.4 26.2 %reduce-scatter.27.cloned.1.call-done = bf16[512,768]{1,0:T(8,128)(2,1)} async-done(((bf16[1024,768]{1,0:T(8,128)(2,1)}), bf16[512,768]{1,0:T(8,128)(2,1)}) %reduce-scatter.27.cloned.1.call-update) | async-done | bytes 786448 | tf_op jit(solution)/shard_map/reduce_scatter | solution.py:307
  668.1 27.3 %all-gather.28.cloned.1.call-done = bf16[1024,768]{1,0:T(8,128)(2,1)} async-done(((bf16[512,768]{1,0:T(8,128)(2,1)}), bf16[1024,768]{1,0:T(8,128)(2,1)}) %all-gather.28.cloned.1.call-update) | async-done | bytes 1572880 | tf_op jit(solution)/shard_map/all_gather | solution.py:271
  695.4 9.4 convert_reduce_fusion.1
  710.5 26.0 %reduce-scatter.29.cloned.1.call-done = bf16[512,768]{1,0:T(8,128)(2,1)} async-done(((bf16[1024,768]{1,0:T(8,128)(2,1)}), bf16[512,768]{1,0:T(8,128)(2,1)}) %reduce-scatter.29.cloned.1.call-update) | async-done | bytes 786448 | tf_op jit(solution)/shard_map/reduce_scatter | solution.py:277
  743.8 26.1 %all-gather.30.cloned.1.call-done = bf16[1024,768]{1,0:T(8,128)(2,1)} async-done(((bf16[512,768]{1,0:T(8,128)(2,1)}), bf16[1024,768]{1,0:T(8,128)(2,1)}) %all-gather.30.cloned.1.call-update) | async-done | bytes 1572880 | tf_op jit(solution)/shard_map/all_gather | solution.py:286
  773.2 11.2 multiply_reduce_fusion.3
  785.8 6.7 multiply_convert_fusion.3
  796.7 6.3 fusion.16
  803.1 9.5 multiply_reduce_fusion.2
  816.3 10.0 multiply_convert_fusion.2
  834.8 26.2 %reduce-scatter.31.cloned.1.call-done = bf16[512,768]{1,0:T(8,128)(2,1)} async-done(((bf16[1024,768]{1,0:T(8,128)(2,1)}), bf16[512,768]{1,0:T(8,128)(2,1)}) %reduce-scatter.31.cloned.1.call-update) | async-done | bytes 786448 | tf_op jit(solution)/shard_map/reduce_scatter | solution.py:307
  873.4 27.3 %all-gather.32.cloned.1.call-done = bf16[1024,768]{1,0:T(8,128)(2,1)} async-done(((bf16[512,768]{1,0:T(8,128)(2,1)}), bf16[1024,768]{1,0:T(8,128)(2,1)}) %all-gather.32.cloned.1.call-update) | async-done | bytes 1572880 | tf_op jit(solution)/shard_map/all_gather | solution.py:271
  900.7 9.4 convert_reduce_fusion
  916.4 25.4 %reduce-scatter.33.cloned.1.call-done = bf16[512,768]{1,0:T(8,128)(2,1)} async-done(((bf16[1024,768]{1,0:T(8,128)(2,1)}), bf16[512,768]{1,0:T(8,128)(2,1)}) %reduce-scatter.33.cloned.1.call-update) | async-done | bytes 786448 | tf_op jit(solution)/shard_map/reduce_scatter | solution.py:277
  944.9 4.1 convert_reduce_fusion.15
  954.6 8.3 fusion.158
  963.0 9.5 fusion.216
  972.6 4.5 fusion.309
  981.8 4.4 fusion.311
  986.2 4.4 fusion.310
  999.0 11.6 multiply_reduce_fusion.1
  1011.3 6.7 multiply_convert_fusion.1
  1020.2 9.5 multiply_reduce_fusion
  1029.7 12.2 multiply_convert_fusion
  1041.9 4.8 fusion.306
  1051.5 6.5 fusion.12
  1065.7 10.2 add_bitcast_fusion.1
  1075.9 12.0 add_bitcast_fusion
  1092.0 5.2 copy.23
  1106.1 23.8 %all-reduce.1 = (f32[1,2,384]{2,1,0:T(2,128)}, f32[1,1536]{1,0:T(1,128)}) all-reduce(f32[1,2,384]{2,1,0:T(2,128)S(1)} %fusion.263, f32[1,1536]{1,0:T(1,128)S(1)} %broadcast_in_dim.102), channel_id=1, replica_groups=mesh['section'=2,'tensor'=2,'dp'=8] {'dp'}, use_global_device_ids=true, to_apply=%region_61.62 | all-reduce | flops 2304 | bytes 18432 | tf_op jit(solution)/shard_map/psum | solution.py:355
  1132.2 76.4 %all-reduce = (f32[1,2,768]{2,1,0:T(2,128)}, f32[1,4,768]{2,1,0:T(4,128)}) all-reduce(f32[1,2,768]{2,1,0:T(2,128)S(1)} %fusion.261, f32[1,4,768]{2,1,0:T(4,128)S(1)} %fusion.259), channel_id=1, replica_groups=mesh['section'=2,'tensor'=2,'dp'=8] {'tensor','dp'}, use_global_device_ids=true, to_apply=%region_75.76 | all-reduce | flops 4608 | bytes 36864 | tf_op jit(solution)/shard_map/psum | solution.py:358
  1212.6 330.6 %all-reduce.5.cloned.1.call-done = (f32[1,768,3,384]{1,3,2,0:T(8,128)}, f32[1,384,768]{2,1,0:T(8,128)}, f32[1,768,1536]{2,1,0:T(8,128)}, f32[1,1536,768]{2,1,0:T(8,128)}) async-done(((f32[1,768,3,384]{1,3,2,0:T(8,128)}, f32[1,384,768]{2,1,0:T(8,128)}, f32[1,768,1536]{2,1,0:T(8,128)}, f32[1,1536,768]{2,1,0:T(8,128)}), (f32[1,768,3,384]{1,3,2,0:T(8,128)}, f32[1,384,768]{2,1,0:T(8,128)}, ...) | async-done | bytes 14155792 | tf_op jit(solution)/shard_map/psum | solution.py:355
  1543.3 5.2 copy.24
  1549.6 5.5 copy.30
  (743 shorter events, 285.3 us)
Async XLA Ops:
  7.2 128.2 %copy-start = (bf16[1,768,1536]{2,1,0:T(8,128)(2,1)S(1)}, bf16[1,768,1536]{2,1,0:T(8,128)(2,1)}, u32[]{:S(2)}) copy-start(bf16[1,768,1536]{2,1,0:T(8,128)(2,1)} %param.19) | copy-start | bytes 7077892
  7.2 37.1 %all-gather.14.cloned.1.call-start = ((), (), s32[]{:S(2)}) async-start(), calls=%async_computation.12 | async-start | bytes 2359296 | tf_op jit(solution)/shard_map/all_gather | solution.py:151
  11.7 94.8 %copy-start.134 = (f32[768]{0:T(1024)}, f32[768]{0:T(1024)S(1)}, u32[]{:S(2)}) copy-start(f32[768]{0:T(1024)S(1)} %get-tuple-element.45) | copy-start | bytes 9220
  11.7 161.6 %copy-start.149 = (f32[768]{0:T(1024)}, f32[768]{0:T(1024)S(1)}, u32[]{:S(2)}) copy-start(f32[768]{0:T(1024)S(1)} %get-tuple-element.44) | copy-start | bytes 9220
  11.8 167.9 %copy-start.137 = (f32[768]{0:T(1024)}, f32[768]{0:T(1024)S(1)}, u32[]{:S(2)}) copy-start(f32[768]{0:T(1024)S(1)} %get-tuple-element.47) | copy-start | bytes 9220
  11.8 852.0 %copy-start.110 = (f32[768]{0:T(1024)}, f32[768]{0:T(1024)S(1)}, u32[]{:S(2)}) copy-start(f32[768]{0:T(1024)S(1)} %get-tuple-element.155) | copy-start | bytes 9220
  14.2 88.5 %reduce-scatter.13.cloned.1.call-start = ((), (), s32[]{:S(2)}) async-start(), calls=%async_computation.13 | async-start | bytes 2359296 | tf_op jit(solution)/shard_map/reduce_scatter | solution.py:179
  14.3 198.2 %copy-start.180 = (f32[384]{0:T(512)}, f32[384]{0:T(512)S(1)}, u32[]{:S(2)}) copy-start(f32[384]{0:T(512)S(1)} %get-tuple-element.50) | copy-start | bytes 4612
  18.2 162.8 %copy-start.174 = (s32[512]{0:T(512)}, s32[512]{0:T(512)S(1)}, u32[]{:S(2)}) copy-start(s32[512]{0:T(512)S(1)} %iota_add_fusion) | copy-start | bytes 6148
  18.9 162.1 %copy-start.164 = (s32[1,1024]{1,0:T(1,128)}, s32[1,1024]{1,0:T(1,128)S(1)}, u32[]{:S(2)}) copy-start(s32[1,1024]{1,0:T(1,128)S(1)} %get-tuple-element.105) | copy-start | bytes 12292
  20.0 38.0 %copy-start.29 = (pred[512,1024]{1,0:T(8,128)(4,1)}, pred[512,1024]{1,0:T(8,128)(4,1)S(1)}, u32[]{:S(2)}) copy-start(pred[512,1024]{1,0:T(8,128)(4,1)S(1)} %get-tuple-element.115) | copy-start | bytes 1572868
  20.0 48.9 %copy-start.27 = (pred[512,1024]{1,0:T(8,128)(4,1)}, pred[512,1024]{1,0:T(8,128)(4,1)S(1)}, u32[]{:S(2)}) copy-start(pred[512,1024]{1,0:T(8,128)(4,1)S(1)} %get-tuple-element.114) | copy-start | bytes 1572868
  76.5 58.9 %all-gather.16.cloned.1.call-start = ((), (), s32[]{:S(2)}) async-start(), calls=%async_computation.14 | async-start | bytes 2359296 | tf_op jit(solution)/shard_map/all_gather | solution.py:191
  106.5 33.0 %copy-start.170 = (f32[512]{0:T(512)}, f32[512]{0:T(512)S(1)}, u32[]{:S(2)}) copy-start(f32[512]{0:T(512)S(1)} %add_rsqrt_fusion.4) | copy-start | bytes 6148
  108.0 65.3 %reduce-scatter.15.cloned.1.call-start = ((), (), s32[]{:S(2)}) async-start(), calls=%async_computation.15 | async-start | bytes 2359296 | tf_op jit(solution)/shard_map/reduce_scatter | solution.py:196
  108.1 31.4 %copy-start.202 = (f32[1536]{0:T(1024)}, f32[1536]{0:T(1024)S(1)}, u32[]{:S(2)}) copy-start(f32[1536]{0:T(1024)S(1)} %convert_reduce_fusion.24) | copy-start | bytes 18436
  147.1 61.2 %all-gather.18.cloned.1.call-start = ((), (), s32[]{:S(2)}) async-start(), calls=%async_computation.16 | async-start | bytes 2359296 | tf_op jit(solution)/shard_map/all_gather | solution.py:151
  175.3 3.6 collective-permute-start
  179.3 156.0 %copy-start.9 = (bf16[512,768]{1,0:T(8,128)(2,1)}, bf16[512,768]{1,0:T(8,128)(2,1)S(1)}, u32[]{:S(2)}) copy-start(bf16[512,768]{1,0:T(8,128)(2,1)S(1)} %get-tuple-element.88) | copy-start | bytes 2359300
  179.3 33.1 %copy-start.152 = (f32[512]{0:T(512)}, f32[512]{0:T(512)S(1)}, u32[]{:S(2)}) copy-start(f32[512]{0:T(512)S(1)} %broadcast_multiply_fusion.15) | copy-start | bytes 6148
  179.7 32.7 %copy-start.166 = (f32[512]{0:T(512)}, f32[512]{0:T(512)S(1)}, u32[]{:S(2)}) copy-start(f32[512]{0:T(512)S(1)} %add_rsqrt_fusion.3) | copy-start | bytes 6148
  180.9 83.9 %reduce-scatter.17.cloned.1.call-start = ((), (), s32[]{:S(2)}) async-start(), calls=%async_computation.17 | async-start | bytes 2359296 | tf_op jit(solution)/shard_map/reduce_scatter | solution.py:179
  238.6 58.2 %all-gather.20.cloned.1.call-start = ((), (), s32[]{:S(2)}) async-start(), calls=%async_computation.18 | async-start | bytes 2359296 | tf_op jit(solution)/shard_map/all_gather | solution.py:191
  266.4 30.4 %copy-start.203 = (f32[1536]{0:T(1024)S(1)}, f32[1536]{0:T(1024)}, u32[]{:S(2)}) copy-start(f32[1536]{0:T(1024)} %copy-done.202) | copy-start | bytes 18436
  268.0 35.6 %copy-start.172 = (f32[512]{0:T(512)}, f32[512]{0:T(512)S(1)}, u32[]{:S(2)}) copy-start(f32[512]{0:T(512)S(1)} %add_rsqrt_fusion.2) | copy-start | bytes 6148
  269.4 65.8 %reduce-scatter.19.cloned.1.call-start = ((), (), s32[]{:S(2)}) async-start(), calls=%async_computation.19 | async-start | bytes 2359296 | tf_op jit(solution)/shard_map/reduce_scatter | solution.py:196
  305.3 29.9 %copy-start.150 = (f32[768]{0:T(1024)S(1)}, f32[768]{0:T(1024)}, u32[]{:S(2)}) copy-start(f32[768]{0:T(1024)} %copy-done.149) | copy-start | bytes 9220
  309.0 62.4 %all-gather.22.cloned.1.call-start = ((), (), s32[]{:S(2)}) async-start(), calls=%async_computation.20 | async-start | bytes 2359296 | tf_op jit(solution)/shard_map/all_gather | solution.py:151
  338.4 3.5 collective-permute-start.1
  342.3 317.0 %copy-start.7 = (bf16[512,768]{1,0:T(8,128)(2,1)}, bf16[512,768]{1,0:T(8,128)(2,1)S(1)}, u32[]{:S(2)}) copy-start(bf16[512,768]{1,0:T(8,128)(2,1)S(1)} %get-tuple-element.86) | copy-start | bytes 2359300
  342.3 33.1 %copy-start.160 = (f32[512]{0:T(512)}, f32[512]{0:T(512)S(1)}, u32[]{:S(2)}) copy-start(f32[512]{0:T(512)S(1)} %broadcast_multiply_fusion.13) | copy-start | bytes 6148
  342.7 32.7 %copy-start.176 = (f32[512]{0:T(512)}, f32[512]{0:T(512)S(1)}, u32[]{:S(2)}) copy-start(f32[512]{0:T(512)S(1)} %add_rsqrt_fusion.1) | copy-start | bytes 6148
  344.0 84.4 %reduce-scatter.21.cloned.1.call-start = ((), (), s32[]{:S(2)}) async-start(), calls=%async_computation.21 | async-start | bytes 2359296 | tf_op jit(solution)/shard_map/reduce_scatter | solution.py:179
  402.1 30.0 %copy-start.136 = (f32[768]{0:T(1024)S(1)}, f32[768]{0:T(1024)}, u32[]{:S(2)}) copy-start(f32[768]{0:T(1024)} %copy-done.134) | copy-start | bytes 9220
  402.1 58.7 %all-gather.24.cloned.1.call-start = ((), (), s32[]{:S(2)}) async-start(), calls=%async_computation.22 | async-start | bytes 2359296 | tf_op jit(solution)/shard_map/all_gather | solution.py:191
  433.4 56.7 %all-gather.36.cloned.1.call-start = ((), (), s32[]{:S(2)}) async-start(), calls=%async_computation.35 | async-start | bytes 2359296 | tf_op jit(solution)/shard_map/all_gather | solution.py:271
  436.3 94.9 %reduce-scatter.25.cloned.1.call-start = ((), (), s32[]{:S(2)}) async-start(), calls=%async_computation.24 | async-start | bytes 2359296 | tf_op jit(solution)/shard_map/reduce_scatter | solution.py:277
  501.2 30.0 %copy-start.163 = (f32[512]{0:T(512)S(1)}, f32[512]{0:T(512)}, u32[]{:S(2)}) copy-start(f32[512]{0:T(512)} %copy-done.162) | copy-start | bytes 6148
  505.0 60.3 %all-gather.26.cloned.1.call-start = ((), (), s32[]{:S(2)}) async-start(), calls=%async_computation.25 | async-start | bytes 2359296 | tf_op jit(solution)/shard_map/all_gather | solution.py:286
  537.9 118.7 %reduce-scatter.27.cloned.1.call-start = ((), (), s32[]{:S(2)}) async-start(), calls=%async_computation.26 | async-start | bytes 2359296 | tf_op jit(solution)/shard_map/reduce_scatter | solution.py:307
  626.9 29.7 %copy-start.177 = (f32[512]{0:T(512)S(1)}, f32[512]{0:T(512)}, u32[]{:S(2)}) copy-start(f32[512]{0:T(512)} %copy-done.176) | copy-start | bytes 6148
  630.3 65.1 %all-gather.28.cloned.1.call-start = ((), (), s32[]{:S(2)}) async-start(), calls=%async_computation.27 | async-start | bytes 2359296 | tf_op jit(solution)/shard_map/all_gather | solution.py:271
  662.0 33.4 %copy-start.204 = (f32[1536]{0:T(1024)S(1)}, f32[1536]{0:T(1024)}, u32[]{:S(2)}) copy-start(f32[1536]{0:T(1024)} %copy-done.202) | copy-start | bytes 18436
  662.0 4.3 collective-permute-start.2
  668.1 68.4 %reduce-scatter.29.cloned.1.call-start = ((), (), s32[]{:S(2)}) async-start(), calls=%async_computation.28 | async-start | bytes 2359296 | tf_op jit(solution)/shard_map/reduce_scatter | solution.py:277
  706.5 30.0 %copy-start.10 = (bf16[512,768]{1,0:T(8,128)(2,1)S(1)}, bf16[512,768]{1,0:T(8,128)(2,1)}, u32[]{:S(2)}) copy-start(bf16[512,768]{1,0:T(8,128)(2,1)} %copy-done.9) | copy-start | bytes 2359300
  706.5 30.0 %copy-start.159 = (f32[512]{0:T(512)S(1)}, f32[512]{0:T(512)}, u32[]{:S(2)}) copy-start(f32[512]{0:T(512)} %copy-done.158) | copy-start | bytes 6148
  706.5 30.0 %copy-start.173 = (f32[512]{0:T(512)S(1)}, f32[512]{0:T(512)}, u32[]{:S(2)}) copy-start(f32[512]{0:T(512)} %copy-done.172) | copy-start | bytes 6148
  710.3 59.6 %all-gather.30.cloned.1.call-start = ((), (), s32[]{:S(2)}) async-start(), calls=%async_computation.29 | async-start | bytes 2359296 | tf_op jit(solution)/shard_map/all_gather | solution.py:286
  742.5 118.5 %reduce-scatter.31.cloned.1.call-start = ((), (), s32[]{:S(2)}) async-start(), calls=%async_computation.30 | async-start | bytes 2359296 | tf_op jit(solution)/shard_map/reduce_scatter | solution.py:307
  831.3 29.7 %copy-start.153 = (f32[512]{0:T(512)S(1)}, f32[512]{0:T(512)}, u32[]{:S(2)}) copy-start(f32[512]{0:T(512)} %copy-done.152) | copy-start | bytes 6148
  831.3 29.7 %copy-start.167 = (f32[512]{0:T(512)S(1)}, f32[512]{0:T(512)}, u32[]{:S(2)}) copy-start(f32[512]{0:T(512)} %copy-done.166) | copy-start | bytes 6148
  834.8 65.9 %all-gather.32.cloned.1.call-start = ((), (), s32[]{:S(2)}) async-start(), calls=%async_computation.31 | async-start | bytes 2359296 | tf_op jit(solution)/shard_map/all_gather | solution.py:271
  866.6 34.1 %copy-start.205 = (f32[1536]{0:T(1024)S(1)}, f32[1536]{0:T(1024)}, u32[]{:S(2)}) copy-start(f32[1536]{0:T(1024)} %copy-done.202) | copy-start | bytes 18436
  867.5 4.2 collective-permute-start.3
  873.3 68.5 %reduce-scatter.33.cloned.1.call-start = ((), (), s32[]{:S(2)}) async-start(), calls=%async_computation.32 | async-start | bytes 2359296 | tf_op jit(solution)/shard_map/reduce_scatter | solution.py:277
  911.8 30.0 %copy-start.18 = (bf16[512,768]{1,0:T(8,128)(2,1)S(1)}, bf16[512,768]{1,0:T(8,128)(2,1)}, u32[]{:S(2)}) copy-start(bf16[512,768]{1,0:T(8,128)(2,1)} %reduce-scatter.13.cloned.1.call-done) | copy-start | bytes 2359300
  911.8 30.0 %copy-start.157 = (f32[512]{0:T(512)S(1)}, f32[512]{0:T(512)}, u32[]{:S(2)}) copy-start(f32[512]{0:T(512)} %copy-done.156) | copy-start | bytes 6148
  911.8 30.0 %copy-start.171 = (f32[512]{0:T(512)S(1)}, f32[512]{0:T(512)}, u32[]{:S(2)}) copy-start(f32[512]{0:T(512)} %copy-done.170) | copy-start | bytes 6148
  915.5 80.9 %all-gather.34.cloned.1.call-start = ((), (), s32[]{:S(2)}) async-start(), calls=%async_computation.33 | async-start | bytes 2359296 | tf_op jit(solution)/shard_map/all_gather | solution.py:286
  949.1 152.4 %reduce-scatter.23.cloned.1.call-start = ((), (), s32[]{:S(2)}) async-start(), calls=%async_computation.23 | async-start | bytes 2359296 | tf_op jit(solution)/shard_map/reduce_scatter | solution.py:196
  962.9 166.9 %reduce-scatter.35.cloned.1.call-start = ((), (), s32[]{:S(2)}) async-start(), calls=%async_computation.34 | async-start | bytes 2359296 | tf_op jit(solution)/shard_map/reduce_scatter | solution.py:307
  1065.6 477.7 %all-reduce.5.cloned.1.call-start = ((), (), s32[]{:S(2)}) async-start(), calls=%async_computation.36 | async-start | bytes 28311552 | tf_op jit(solution)/shard_map/psum | solution.py:355
  1104.2 104.4 %copy-start.80 = (bf16[512,768]{1,0:T(8,128)(2,1)S(1)}, bf16[512,768]{1,0:T(8,128)(2,1)}, u32[]{:S(2)}) copy-start(bf16[512,768]{1,0:T(8,128)(2,1)} %copy-done.79) | copy-start | bytes 2359300
  (211 other events, 1125.6 us)
Sparse Core Ops, SparseCore 0:
  14.3 29.8 all-gather.13
  76.6 26.0 reduce-scatter.12
  108.1 27.2 all-gather.15
  147.2 26.0 reduce-scatter.14
  181.1 27.2 all-gather.17
  238.7 26.0 reduce-scatter.16
  269.5 27.2 all-gather.19
  309.1 26.0 reduce-scatter.18
  344.1 27.2 all-gather.21
  402.2 26.0 reduce-scatter.20
  433.6 27.2 all-gather.23
  462.8 27.1 all-gather.35
  505.1 26.0 reduce-scatter.24
  538.0 27.2 all-gather.25
  630.4 26.0 reduce-scatter.26
  668.2 27.2 all-gather.27
  710.4 26.0 reduce-scatter.28
  742.6 27.2 all-gather.29
  834.9 26.0 reduce-scatter.30
  873.4 27.2 all-gather.31
  915.7 26.0 reduce-scatter.32
  949.2 27.2 all-gather.33
  979.2 26.0 reduce-scatter.22
  1065.7 26.1 reduce-scatter.34
  1100.8 442.3 all-reduce.4
where the time goes:
time: 1570 us; the launch traced here: 1560 us
  waiting for transfers between devices  883 us (56%)
  matrix products  325 us (21%)
  other arithmetic  167 us (11%)
  blocking collectives  100 us (6%)
  local copies, waits for them, and re-layouts  62.7 us (4%)
  between operations  17.2 us (1%)
    psum x1, waiting for transfers between devices, local(): lax.psum((g_qkv, g_qv, g_out, g_up, g_upb, g_down), 'dp')  331 us
    all_gather x3, waiting for transfers between devices, local(): lax.all_gather(forward_normed2, 'tensor', axis=0, tiled=True)  79 us
    all_gather x3, waiting for transfers between devices, local(): grad_all = lax.all_gather(grad_branch2, 'tensor', axis=0, tiled=True)  78 us
    reduce_scatter x3, waiting for transfers between devices, local(): lax.psum_scatter(jnp.dot(forward_mixed_rows, out_mat, preferred_element_t...  77.8 us
    reduce_scatter x3, waiting for transfers between devices, local(): lax.psum_scatter(dot_last(grad_hidden, up_mat).astype(jnp.bfloat16), 'ten...  77.6 us
    psum x1, blocking collectives, local(): g_gain, g_shift = lax.psum((g_gain, g_shift), ('tensor', 'dp'))  76.4 us
    all_gather x3, waiting for transfers between devices, local(): lax.all_gather(normed.astype(jnp.bfloat16), 'tensor', axis=0, tiled=True)  75.1 us
    dot_general x6, matrix products, attention_backward(): jnp.einsum('qhd,khd->hqk', part_grad, value_rows, preferred_element_type=...  63 us
  transfers between devices with their start and end apart: 29, of which 26 were waited for; matrix products, arithmetic and copies ran while one was open for 11% of the time, Pallas kernels for 0%

commit v1 on v0

--- a/solution.py
+++ b/solution.py
@@ -1,10 +1,20 @@
+import functools
 import jax
 import jax.numpy as jnp
 from jax import lax
 from jax.sharding import PartitionSpec as P
+from jax.lax import psum
 
 HEAD = 64
 eps_norm = 1e-05
+
+
+def spread_core(chunk, ax_name, net_axis):
+    x_next = psum(psum(chunk, axis_name=net_axis), axis_name=ax_name)
+    return x_next
+
+
+trace_the_array = functools.partial(spread_core, ax_name="tensor", net_axis="dp")
 
 
 def shifted(block, axis, distance):
@@ -355,7 +365,7 @@
     g_qkv, g_qv, g_out, g_up, g_upb, g_down = lax.psum(
         (g_qkv, g_qv, g_out, g_up, g_upb, g_down), "dp"
     )
-    g_gain, g_shift = lax.psum((g_gain, g_shift), ("tensor", "dp"))
+    g_gain, g_shift = trace_the_array((g_gain, g_shift))
     return (
         act_rows[None],
         grad_rows_out[None],

time: 1570 us -> 1570 us (level)
  blocking collectives: 100 us -> 47 us
  waiting for transfers between devices: 883 us -> 935 us
    psum x1, blocking collectives: 76.4 us -> 7.39 us  [spread_core(): x_next = psum(psum(chunk, axis_name=net_axis), axis_name=ax_name)]
    psum x1, waiting for transfers between devices: 331 us -> 382 us  [local(): lax.psum((g_qkv, g_qv, g_out, g_up, g_upb, g_down), 'dp')]
    psum x1, blocking collectives: 23.8 us -> 39.6 us  [local(): lax.psum((g_qkv, g_qv, g_out, g_up, g_upb, g_down), 'dp')]
  transfers between devices with their start and end apart: 29 -> 29, of which waited for: 26 -> 26; matrix products, arithmetic and copies ran while one was open for 11% -> 12% of each run, Pallas kernels for 0% -> 0%
where the time goes in v1:
time: 1570 us; the launch traced here: 1560 us
  waiting for transfers between devices  935 us (60%)
  matrix products  325 us (21%)
  other arithmetic  168 us (11%)
  local copies, waits for them, and re-layouts  62.7 us (4%)
  blocking collectives  47 us (3%)
  between operations  17.2 us (1%)
    psum x1, waiting for transfers between devices, local(): lax.psum((g_qkv, g_qv, g_out, g_up, g_upb, g_down), 'dp')  382 us
    all_gather x3, waiting for transfers between devices, local(): lax.all_gather(forward_normed2, 'tensor', axis=0, tiled=True)  79 us
    all_gather x3, waiting for transfers between devices, local(): grad_all = lax.all_gather(grad_branch2, 'tensor', axis=0, tiled=True)  78 us
    reduce_scatter x3, waiting for transfers between devices, local(): lax.psum_scatter(jnp.dot(forward_mixed_rows, out_mat, preferred_element_t...  77.8 us
    reduce_scatter x3, waiting for transfers between devices, local(): lax.psum_scatter(dot_last(grad_hidden, up_mat).astype(jnp.bfloat16), 'ten...  77.6 us
    all_gather x3, waiting for transfers between devices, local(): lax.all_gather(normed.astype(jnp.bfloat16), 'tensor', axis=0, tiled=True)  75.1 us
    dot_general x6, matrix products, attention_backward(): jnp.einsum('qhd,khd->hqk', part_grad, value_rows, preferred_element_type=...  63 us
    dot_general x12, matrix products, dot_rows(): lax.dot_general(left, right, (((0,), (0,)), ((), ())), preferred_element_...  61.3 us
  transfers between devices with their start and end apart: 29, of which 26 were waited for; matrix products, arithmetic and copies ran while one was open for 12% of the time, Pallas kernels for 0%

profile of v1, /device:TPU:0, one launch (start us, length us, event | category | flops | bytes accessed | tf_op | source)
XLA Modules:
  0.0 1562.3 jit_solution(8378889533231111412)
XLA Ops:
  20.0 24.2 %all-gather.14.cloned.1.call-done = bf16[1024,768]{1,0:T(8,128)(2,1)} async-done(((bf16[512,768]{1,0:T(8,128)(2,1)}), bf16[1024,768]{1,0:T(8,128)(2,1)}) %all-gather.14.cloned.1.call-update) | async-done | bytes 1572880 | tf_op jit(solution)/shard_map/all_gather | solution.py:161
  59.2 4.1 fusion.233
  70.1 4.1 fusion.234
  76.7 26.0 %reduce-scatter.13.cloned.1.call-done = bf16[512,768]{1,0:T(8,128)(2,1)} async-done(((bf16[1024,768]{1,0:T(8,128)(2,1)}), bf16[512,768]{1,0:T(8,128)(2,1)}) %reduce-scatter.13.cloned.1.call-update) | async-done | bytes 786448 | tf_op jit(solution)/shard_map/reduce_scatter | solution.py:189
  108.1 27.3 %all-gather.16.cloned.1.call-done = bf16[1024,768]{1,0:T(8,128)(2,1)} async-done(((bf16[512,768]{1,0:T(8,128)(2,1)}), bf16[1024,768]{1,0:T(8,128)(2,1)}) %all-gather.16.cloned.1.call-update) | async-done | bytes 1572880 | tf_op jit(solution)/shard_map/all_gather | solution.py:201
  135.4 4.1 fusion.97
  142.1 5.0 fusion.152
  147.2 26.2 %reduce-scatter.15.cloned.1.call-done = bf16[512,768]{1,0:T(8,128)(2,1)} async-done(((bf16[1024,768]{1,0:T(8,128)(2,1)}), bf16[512,768]{1,0:T(8,128)(2,1)}) %reduce-scatter.15.cloned.1.call-update) | async-done | bytes 786448 | tf_op jit(solution)/shard_map/reduce_scatter | solution.py:206
  182.9 25.4 %all-gather.18.cloned.1.call-done = bf16[1024,768]{1,0:T(8,128)(2,1)} async-done(((bf16[512,768]{1,0:T(8,128)(2,1)}), bf16[1024,768]{1,0:T(8,128)(2,1)}) %all-gather.18.cloned.1.call-update) | async-done | bytes 1572880 | tf_op jit(solution)/shard_map/all_gather | solution.py:161
  220.6 4.1 fusion.231
  231.5 4.1 fusion.232
  239.0 25.8 %reduce-scatter.17.cloned.1.call-done = bf16[512,768]{1,0:T(8,128)(2,1)} async-done(((bf16[1024,768]{1,0:T(8,128)(2,1)}), bf16[512,768]{1,0:T(8,128)(2,1)}) %reduce-scatter.17.cloned.1.call-update) | async-done | bytes 786448 | tf_op jit(solution)/shard_map/reduce_scatter | solution.py:189
  269.4 27.3 %all-gather.20.cloned.1.call-done = bf16[1024,768]{1,0:T(8,128)(2,1)} async-done(((bf16[512,768]{1,0:T(8,128)(2,1)}), bf16[1024,768]{1,0:T(8,128)(2,1)}) %all-gather.20.cloned.1.call-update) | async-done | bytes 1572880 | tf_op jit(solution)/shard_map/all_gather | solution.py:201
  296.8 6.9 multiply_convert_fusion.7
  309.0 26.2 %reduce-scatter.19.cloned.1.call-done = bf16[512,768]{1,0:T(8,128)(2,1)} async-done(((bf16[1024,768]{1,0:T(8,128)(2,1)}), bf16[512,768]{1,0:T(8,128)(2,1)}) %reduce-scatter.19.cloned.1.call-update) | async-done | bytes 786448 | tf_op jit(solution)/shard_map/reduce_scatter | solution.py:206
  345.9 25.4 %all-gather.22.cloned.1.call-done = bf16[1024,768]{1,0:T(8,128)(2,1)} async-done(((bf16[512,768]{1,0:T(8,128)(2,1)}), bf16[1024,768]{1,0:T(8,128)(2,1)}) %all-gather.22.cloned.1.call-update) | async-done | bytes 1572880 | tf_op jit(solution)/shard_map/all_gather | solution.py:161
  384.1 4.1 fusion.230
  395.0 4.1 fusion.229
  402.3 26.0 %reduce-scatter.21.cloned.1.call-done = bf16[512,768]{1,0:T(8,128)(2,1)} async-done(((bf16[1024,768]{1,0:T(8,128)(2,1)}), bf16[512,768]{1,0:T(8,128)(2,1)}) %reduce-scatter.21.cloned.1.call-update) | async-done | bytes 786448 | tf_op jit(solution)/shard_map/reduce_scatter | solution.py:189
  436.3 24.5 %all-gather.24.cloned.1.call-done = bf16[1024,768]{1,0:T(8,128)(2,1)} async-done(((bf16[512,768]{1,0:T(8,128)(2,1)}), bf16[1024,768]{1,0:T(8,128)(2,1)}) %all-gather.24.cloned.1.call-update) | async-done | bytes 1572880 | tf_op jit(solution)/shard_map/all_gather | solution.py:201
  460.8 5.9 fusion.93
  466.7 23.4 %all-gather.36.cloned.1.call-done = bf16[1,1024,768]{2,1,0:T(8,128)(2,1)} async-done(((bf16[1,512,768]{2,1,0:T(8,128)(2,1)}), bf16[1,1024,768]{2,1,0:T(8,128)(2,1)}) %all-gather.36.cloned.1.call-update) | async-done | bytes 1572880 | tf_op jit(solution)/shard_map/all_gather | solution.py:281
  490.1 9.4 convert_reduce_fusion.2
  505.0 26.2 %reduce-scatter.25.cloned.1.call-done = bf16[512,768]{1,0:T(8,128)(2,1)} async-done(((bf16[1024,768]{1,0:T(8,128)(2,1)}), bf16[512,768]{1,0:T(8,128)(2,1)}) %reduce-scatter.25.cloned.1.call-update) | async-done | bytes 786448 | tf_op jit(solution)/shard_map/reduce_scatter | solution.py:287
  540.6 24.6 %all-gather.26.cloned.1.call-done = bf16[1024,768]{1,0:T(8,128)(2,1)} async-done(((bf16[512,768]{1,0:T(8,128)(2,1)}), bf16[1024,768]{1,0:T(8,128)(2,1)}) %all-gather.26.cloned.1.call-update) | async-done | bytes 1572880 | tf_op jit(solution)/shard_map/all_gather | solution.py:296
  568.5 11.5 multiply_reduce_fusion.5
  581.2 6.7 multiply_convert_fusion.5
  592.2 6.3 fusion.20
  598.5 9.6 multiply_reduce_fusion.4
  611.8 10.1 multiply_convert_fusion.4
  630.4 26.2 %reduce-scatter.27.cloned.1.call-done = bf16[512,768]{1,0:T(8,128)(2,1)} async-done(((bf16[1024,768]{1,0:T(8,128)(2,1)}), bf16[512,768]{1,0:T(8,128)(2,1)}) %reduce-scatter.27.cloned.1.call-update) | async-done | bytes 786448 | tf_op jit(solution)/shard_map/reduce_scatter | solution.py:317
  668.1 27.3 %all-gather.28.cloned.1.call-done = bf16[1024,768]{1,0:T(8,128)(2,1)} async-done(((bf16[512,768]{1,0:T(8,128)(2,1)}), bf16[1024,768]{1,0:T(8,128)(2,1)}) %all-gather.28.cloned.1.call-update) | async-done | bytes 1572880 | tf_op jit(solution)/shard_map/all_gather | solution.py:281
  695.4 9.4 convert_reduce_fusion.1
  710.5 26.0 %reduce-scatter.29.cloned.1.call-done = bf16[512,768]{1,0:T(8,128)(2,1)} async-done(((bf16[1024,768]{1,0:T(8,128)(2,1)}), bf16[512,768]{1,0:T(8,128)(2,1)}) %reduce-scatter.29.cloned.1.call-update) | async-done | bytes 786448 | tf_op jit(solution)/shard_map/reduce_scatter | solution.py:287
  743.8 26.1 %all-gather.30.cloned.1.call-done = bf16[1024,768]{1,0:T(8,128)(2,1)} async-done(((bf16[512,768]{1,0:T(8,128)(2,1)}), bf16[1024,768]{1,0:T(8,128)(2,1)}) %all-gather.30.cloned.1.call-update) | async-done | bytes 1572880 | tf_op jit(solution)/shard_map/all_gather | solution.py:296
  773.2 11.2 multiply_reduce_fusion.3
  785.8 6.7 multiply_convert_fusion.3
  796.7 6.3 fusion.16
  803.1 9.5 multiply_reduce_fusion.2
  816.3 10.0 multiply_convert_fusion.2
  834.8 26.2 %reduce-scatter.31.cloned.1.call-done = bf16[512,768]{1,0:T(8,128)(2,1)} async-done(((bf16[1024,768]{1,0:T(8,128)(2,1)}), bf16[512,768]{1,0:T(8,128)(2,1)}) %reduce-scatter.31.cloned.1.call-update) | async-done | bytes 786448 | tf_op jit(solution)/shard_map/reduce_scatter | solution.py:317
  873.4 27.3 %all-gather.32.cloned.1.call-done = bf16[1024,768]{1,0:T(8,128)(2,1)} async-done(((bf16[512,768]{1,0:T(8,128)(2,1)}), bf16[1024,768]{1,0:T(8,128)(2,1)}) %all-gather.32.cloned.1.call-update) | async-done | bytes 1572880 | tf_op jit(solution)/shard_map/all_gather | solution.py:281
  900.7 9.4 convert_reduce_fusion
  916.4 25.4 %reduce-scatter.33.cloned.1.call-done = bf16[512,768]{1,0:T(8,128)(2,1)} async-done(((bf16[1024,768]{1,0:T(8,128)(2,1)}), bf16[512,768]{1,0:T(8,128)(2,1)}) %reduce-scatter.33.cloned.1.call-update) | async-done | bytes 786448 | tf_op jit(solution)/shard_map/reduce_scatter | solution.py:287
  944.9 4.1 convert_reduce_fusion.15
  954.6 8.3 fusion.158
  963.0 9.5 fusion.216
  972.6 4.5 fusion.307
  981.8 4.4 fusion.309
  986.2 4.4 fusion.308
  999.0 11.6 multiply_reduce_fusion.1
  1011.3 6.7 multiply_convert_fusion.1
  1020.2 9.5 multiply_reduce_fusion
  1029.7 12.2 multiply_convert_fusion
  1041.9 4.8 fusion.304
  1051.5 6.5 fusion.12
  1065.7 10.2 add_bitcast_fusion.1
  1075.9 12.0 add_bitcast_fusion
  1092.0 5.2 copy.23
  1109.0 39.6 %all-reduce = (f32[1,2,384]{2,1,0:T(2,128)}, f32[1,1536]{1,0:T(1,128)}, f32[2,768]{1,0:T(2,128)S(1)}, f32[4,768]{1,0:T(4,128)S(1)}) all-reduce(f32[1,2,384]{2,1,0:T(2,128)S(1)} %fusion.261, f32[1,1536]{1,0:T(1,128)S(1)} %broadcast_in_dim.102, f32[2,768]{1,0:T(2,128)S(1)} %fusion.259, ...), channel_id=1, replica_groups=mesh['section'=2,'tensor'=2,'dp'=8] {'dp'}, use_global_device_ids=true, to_apply=%region_61.62 | all-reduce | flops 6912 | bytes 55296 | tf_op jit(solution)/shard_map/psum | solution.py:365
  1148.5 7.4 all-reduce.2
  1159.9 381.7 %all-reduce.5.cloned.1.call-done = (f32[1,768,3,384]{1,3,2,0:T(8,128)}, f32[1,384,768]{2,1,0:T(8,128)}, f32[1,768,1536]{2,1,0:T(8,128)}, f32[1,1536,768]{2,1,0:T(8,128)}) async-done(((f32[1,768,3,384]{1,3,2,0:T(8,128)}, f32[1,384,768]{2,1,0:T(8,128)}, f32[1,768,1536]{2,1,0:T(8,128)}, f32[1,1536,768]{2,1,0:T(8,128)}), (f32[1,768,3,384]{1,3,2,0:T(8,128)}, f32[1,384,768]{2,1,0:T(8,128)}, ...) | async-done | bytes 14155792 | tf_op jit(solution)/shard_map/psum | solution.py:365
  1541.6 5.2 copy.24
  1547.9 5.5 copy.30
  (743 shorter events, 285.8 us)
Async XLA Ops:
  7.2 128.2 %copy-start = (bf16[1,768,1536]{2,1,0:T(8,128)(2,1)S(1)}, bf16[1,768,1536]{2,1,0:T(8,128)(2,1)}, u32[]{:S(2)}) copy-start(bf16[1,768,1536]{2,1,0:T(8,128)(2,1)} %param.19) | copy-start | bytes 7077892
  7.2 37.1 %all-gather.14.cloned.1.call-start = ((), (), s32[]{:S(2)}) async-start(), calls=%async_computation.12 | async-start | bytes 2359296 | tf_op jit(solution)/shard_map/all_gather | solution.py:161
  11.7 94.8 %copy-start.134 = (f32[768]{0:T(1024)}, f32[768]{0:T(1024)S(1)}, u32[]{:S(2)}) copy-start(f32[768]{0:T(1024)S(1)} %get-tuple-element.45) | copy-start | bytes 9220
  11.7 161.6 %copy-start.149 = (f32[768]{0:T(1024)}, f32[768]{0:T(1024)S(1)}, u32[]{:S(2)}) copy-start(f32[768]{0:T(1024)S(1)} %get-tuple-element.44) | copy-start | bytes 9220
  11.8 167.9 %copy-start.137 = (f32[768]{0:T(1024)}, f32[768]{0:T(1024)S(1)}, u32[]{:S(2)}) copy-start(f32[768]{0:T(1024)S(1)} %get-tuple-element.47) | copy-start | bytes 9220
  11.8 852.0 %copy-start.110 = (f32[768]{0:T(1024)}, f32[768]{0:T(1024)S(1)}, u32[]{:S(2)}) copy-start(f32[768]{0:T(1024)S(1)} %get-tuple-element.157) | copy-start | bytes 9220
  14.2 88.5 %reduce-scatter.13.cloned.1.call-start = ((), (), s32[]{:S(2)}) async-start(), calls=%async_computation.13 | async-start | bytes 2359296 | tf_op jit(solution)/shard_map/reduce_scatter | solution.py:189
  14.3 198.2 %copy-start.180 = (f32[384]{0:T(512)}, f32[384]{0:T(512)S(1)}, u32[]{:S(2)}) copy-start(f32[384]{0:T(512)S(1)} %get-tuple-element.50) | copy-start | bytes 4612
  18.2 162.8 %copy-start.174 = (s32[512]{0:T(512)}, s32[512]{0:T(512)S(1)}, u32[]{:S(2)}) copy-start(s32[512]{0:T(512)S(1)} %iota_add_fusion) | copy-start | bytes 6148
  18.9 162.1 %copy-start.164 = (s32[1,1024]{1,0:T(1,128)}, s32[1,1024]{1,0:T(1,128)S(1)}, u32[]{:S(2)}) copy-start(s32[1,1024]{1,0:T(1,128)S(1)} %get-tuple-element.107) | copy-start | bytes 12292
  20.0 38.0 %copy-start.29 = (pred[512,1024]{1,0:T(8,128)(4,1)}, pred[512,1024]{1,0:T(8,128)(4,1)S(1)}, u32[]{:S(2)}) copy-start(pred[512,1024]{1,0:T(8,128)(4,1)S(1)} %get-tuple-element.117) | copy-start | bytes 1572868
  20.0 48.9 %copy-start.27 = (pred[512,1024]{1,0:T(8,128)(4,1)}, pred[512,1024]{1,0:T(8,128)(4,1)S(1)}, u32[]{:S(2)}) copy-start(pred[512,1024]{1,0:T(8,128)(4,1)S(1)} %get-tuple-element.116) | copy-start | bytes 1572868
  76.5 58.9 %all-gather.16.cloned.1.call-start = ((), (), s32[]{:S(2)}) async-start(), calls=%async_computation.14 | async-start | bytes 2359296 | tf_op jit(solution)/shard_map/all_gather | solution.py:201
  106.5 33.0 %copy-start.170 = (f32[512]{0:T(512)}, f32[512]{0:T(512)S(1)}, u32[]{:S(2)}) copy-start(f32[512]{0:T(512)S(1)} %add_rsqrt_fusion.4) | copy-start | bytes 6148
  108.0 65.3 %reduce-scatter.15.cloned.1.call-start = ((), (), s32[]{:S(2)}) async-start(), calls=%async_computation.15 | async-start | bytes 2359296 | tf_op jit(solution)/shard_map/reduce_scatter | solution.py:206
  108.1 31.4 %copy-start.202 = (f32[1536]{0:T(1024)}, f32[1536]{0:T(1024)S(1)}, u32[]{:S(2)}) copy-start(f32[1536]{0:T(1024)S(1)} %convert_reduce_fusion.24) | copy-start | bytes 18436
  147.1 61.2 %all-gather.18.cloned.1.call-start = ((), (), s32[]{:S(2)}) async-start(), calls=%async_computation.16 | async-start | bytes 2359296 | tf_op jit(solution)/shard_map/all_gather | solution.py:161
  175.3 3.6 collective-permute-start
  179.3 156.0 %copy-start.9 = (bf16[512,768]{1,0:T(8,128)(2,1)}, bf16[512,768]{1,0:T(8,128)(2,1)S(1)}, u32[]{:S(2)}) copy-start(bf16[512,768]{1,0:T(8,128)(2,1)S(1)} %get-tuple-element.90) | copy-start | bytes 2359300
  179.3 33.1 %copy-start.152 = (f32[512]{0:T(512)}, f32[512]{0:T(512)S(1)}, u32[]{:S(2)}) copy-start(f32[512]{0:T(512)S(1)} %broadcast_multiply_fusion.15) | copy-start | bytes 6148
  179.7 32.7 %copy-start.166 = (f32[512]{0:T(512)}, f32[512]{0:T(512)S(1)}, u32[]{:S(2)}) copy-start(f32[512]{0:T(512)S(1)} %add_rsqrt_fusion.3) | copy-start | bytes 6148
  180.9 83.9 %reduce-scatter.17.cloned.1.call-start = ((), (), s32[]{:S(2)}) async-start(), calls=%async_computation.17 | async-start | bytes 2359296 | tf_op jit(solution)/shard_map/reduce_scatter | solution.py:189
  238.6 58.2 %all-gather.20.cloned.1.call-start = ((), (), s32[]{:S(2)}) async-start(), calls=%async_computation.18 | async-start | bytes 2359296 | tf_op jit(solution)/shard_map/all_gather | solution.py:201
  266.4 30.4 %copy-start.203 = (f32[1536]{0:T(1024)S(1)}, f32[1536]{0:T(1024)}, u32[]{:S(2)}) copy-start(f32[1536]{0:T(1024)} %copy-done.202) | copy-start | bytes 18436
  268.0 35.6 %copy-start.172 = (f32[512]{0:T(512)}, f32[512]{0:T(512)S(1)}, u32[]{:S(2)}) copy-start(f32[512]{0:T(512)S(1)} %add_rsqrt_fusion.2) | copy-start | bytes 6148
  269.4 65.8 %reduce-scatter.19.cloned.1.call-start = ((), (), s32[]{:S(2)}) async-start(), calls=%async_computation.19 | async-start | bytes 2359296 | tf_op jit(solution)/shard_map/reduce_scatter | solution.py:206
  305.3 29.9 %copy-start.150 = (f32[768]{0:T(1024)S(1)}, f32[768]{0:T(1024)}, u32[]{:S(2)}) copy-start(f32[768]{0:T(1024)} %copy-done.149) | copy-start | bytes 9220
  309.0 62.4 %all-gather.22.cloned.1.call-start = ((), (), s32[]{:S(2)}) async-start(), calls=%async_computation.20 | async-start | bytes 2359296 | tf_op jit(solution)/shard_map/all_gather | solution.py:161
  338.4 3.5 collective-permute-start.1
  342.3 317.0 %copy-start.7 = (bf16[512,768]{1,0:T(8,128)(2,1)}, bf16[512,768]{1,0:T(8,128)(2,1)S(1)}, u32[]{:S(2)}) copy-start(bf16[512,768]{1,0:T(8,128)(2,1)S(1)} %get-tuple-element.88) | copy-start | bytes 2359300
  342.3 33.1 %copy-start.160 = (f32[512]{0:T(512)}, f32[512]{0:T(512)S(1)}, u32[]{:S(2)}) copy-start(f32[512]{0:T(512)S(1)} %broadcast_multiply_fusion.13) | copy-start | bytes 6148
  342.7 32.7 %copy-start.176 = (f32[512]{0:T(512)}, f32[512]{0:T(512)S(1)}, u32[]{:S(2)}) copy-start(f32[512]{0:T(512)S(1)} %add_rsqrt_fusion.1) | copy-start | bytes 6148
  344.0 84.4 %reduce-scatter.21.cloned.1.call-start = ((), (), s32[]{:S(2)}) async-start(), calls=%async_computation.21 | async-start | bytes 2359296 | tf_op jit(solution)/shard_map/reduce_scatter | solution.py:189
  402.1 30.0 %copy-start.136 = (f32[768]{0:T(1024)S(1)}, f32[768]{0:T(1024)}, u32[]{:S(2)}) copy-start(f32[768]{0:T(1024)} %copy-done.134) | copy-start | bytes 9220
  402.1 58.7 %all-gather.24.cloned.1.call-start = ((), (), s32[]{:S(2)}) async-start(), calls=%async_computation.22 | async-start | bytes 2359296 | tf_op jit(solution)/shard_map/all_gather | solution.py:201
  433.4 56.7 %all-gather.36.cloned.1.call-start = ((), (), s32[]{:S(2)}) async-start(), calls=%async_computation.35 | async-start | bytes 2359296 | tf_op jit(solution)/shard_map/all_gather | solution.py:281
  436.3 94.9 %reduce-scatter.25.cloned.1.call-start = ((), (), s32[]{:S(2)}) async-start(), calls=%async_computation.24 | async-start | bytes 2359296 | tf_op jit(solution)/shard_map/reduce_scatter | solution.py:287
  501.2 30.0 %copy-start.163 = (f32[512]{0:T(512)S(1)}, f32[512]{0:T(512)}, u32[]{:S(2)}) copy-start(f32[512]{0:T(512)} %copy-done.162) | copy-start | bytes 6148
  505.0 60.3 %all-gather.26.cloned.1.call-start = ((), (), s32[]{:S(2)}) async-start(), calls=%async_computation.25 | async-start | bytes 2359296 | tf_op jit(solution)/shard_map/all_gather | solution.py:296
  537.9 118.7 %reduce-scatter.27.cloned.1.call-start = ((), (), s32[]{:S(2)}) async-start(), calls=%async_computation.26 | async-start | bytes 2359296 | tf_op jit(solution)/shard_map/reduce_scatter | solution.py:317
  626.9 29.7 %copy-start.177 = (f32[512]{0:T(512)S(1)}, f32[512]{0:T(512)}, u32[]{:S(2)}) copy-start(f32[512]{0:T(512)} %copy-done.176) | copy-start | bytes 6148
  630.3 65.1 %all-gather.28.cloned.1.call-start = ((), (), s32[]{:S(2)}) async-start(), calls=%async_computation.27 | async-start | bytes 2359296 | tf_op jit(solution)/shard_map/all_gather | solution.py:281
  662.0 33.4 %copy-start.204 = (f32[1536]{0:T(1024)S(1)}, f32[1536]{0:T(1024)}, u32[]{:S(2)}) copy-start(f32[1536]{0:T(1024)} %copy-done.202) | copy-start | bytes 18436
  662.0 4.3 collective-permute-start.2
  668.1 68.4 %reduce-scatter.29.cloned.1.call-start = ((), (), s32[]{:S(2)}) async-start(), calls=%async_computation.28 | async-start | bytes 2359296 | tf_op jit(solution)/shard_map/reduce_scatter | solution.py:287
  706.5 30.0 %copy-start.10 = (bf16[512,768]{1,0:T(8,128)(2,1)S(1)}, bf16[512,768]{1,0:T(8,128)(2,1)}, u32[]{:S(2)}) copy-start(bf16[512,768]{1,0:T(8,128)(2,1)} %copy-done.9) | copy-start | bytes 2359300
  706.5 30.0 %copy-start.159 = (f32[512]{0:T(512)S(1)}, f32[512]{0:T(512)}, u32[]{:S(2)}) copy-start(f32[512]{0:T(512)} %copy-done.158) | copy-start | bytes 6148
  706.5 30.0 %copy-start.173 = (f32[512]{0:T(512)S(1)}, f32[512]{0:T(512)}, u32[]{:S(2)}) copy-start(f32[512]{0:T(512)} %copy-done.172) | copy-start | bytes 6148
  710.3 59.6 %all-gather.30.cloned.1.call-start = ((), (), s32[]{:S(2)}) async-start(), calls=%async_computation.29 | async-start | bytes 2359296 | tf_op jit(solution)/shard_map/all_gather | solution.py:296
  742.5 118.5 %reduce-scatter.31.cloned.1.call-start = ((), (), s32[]{:S(2)}) async-start(), calls=%async_computation.30 | async-start | bytes 2359296 | tf_op jit(solution)/shard_map/reduce_scatter | solution.py:317
  831.3 29.7 %copy-start.153 = (f32[512]{0:T(512)S(1)}, f32[512]{0:T(512)}, u32[]{:S(2)}) copy-start(f32[512]{0:T(512)} %copy-done.152) | copy-start | bytes 6148
  831.3 29.7 %copy-start.167 = (f32[512]{0:T(512)S(1)}, f32[512]{0:T(512)}, u32[]{:S(2)}) copy-start(f32[512]{0:T(512)} %copy-done.166) | copy-start | bytes 6148
  834.8 65.9 %all-gather.32.cloned.1.call-start = ((), (), s32[]{:S(2)}) async-start(), calls=%async_computation.31 | async-start | bytes 2359296 | tf_op jit(solution)/shard_map/all_gather | solution.py:281
  866.6 34.1 %copy-start.205 = (f32[1536]{0:T(1024)S(1)}, f32[1536]{0:T(1024)}, u32[]{:S(2)}) copy-start(f32[1536]{0:T(1024)} %copy-done.202) | copy-start | bytes 18436
  867.5 4.2 collective-permute-start.3
  873.3 68.5 %reduce-scatter.33.cloned.1.call-start = ((), (), s32[]{:S(2)}) async-start(), calls=%async_computation.32 | async-start | bytes 2359296 | tf_op jit(solution)/shard_map/reduce_scatter | solution.py:287
  911.8 30.0 %copy-start.18 = (bf16[512,768]{1,0:T(8,128)(2,1)S(1)}, bf16[512,768]{1,0:T(8,128)(2,1)}, u32[]{:S(2)}) copy-start(bf16[512,768]{1,0:T(8,128)(2,1)} %reduce-scatter.13.cloned.1.call-done) | copy-start | bytes 2359300
  911.8 30.0 %copy-start.157 = (f32[512]{0:T(512)S(1)}, f32[512]{0:T(512)}, u32[]{:S(2)}) copy-start(f32[512]{0:T(512)} %copy-done.156) | copy-start | bytes 6148
  911.8 30.0 %copy-start.171 = (f32[512]{0:T(512)S(1)}, f32[512]{0:T(512)}, u32[]{:S(2)}) copy-start(f32[512]{0:T(512)} %copy-done.170) | copy-start | bytes 6148
  915.5 80.9 %all-gather.34.cloned.1.call-start = ((), (), s32[]{:S(2)}) async-start(), calls=%async_computation.33 | async-start | bytes 2359296 | tf_op jit(solution)/shard_map/all_gather | solution.py:296
  949.1 152.4 %reduce-scatter.23.cloned.1.call-start = ((), (), s32[]{:S(2)}) async-start(), calls=%async_computation.23 | async-start | bytes 2359296 | tf_op jit(solution)/shard_map/reduce_scatter | solution.py:206
  962.9 143.2 %reduce-scatter.35.cloned.1.call-start = ((), (), s32[]{:S(2)}) async-start(), calls=%async_computation.34 | async-start | bytes 2359296 | tf_op jit(solution)/shard_map/reduce_scatter | solution.py:317
  1065.6 476.0 %all-reduce.5.cloned.1.call-start = ((), (), s32[]{:S(2)}) async-start(), calls=%async_computation.36 | async-start | bytes 28311552 | tf_op jit(solution)/shard_map/psum | solution.py:365
  1104.2 51.7 %copy-start.80 = (bf16[512,768]{1,0:T(8,128)(2,1)S(1)}, bf16[512,768]{1,0:T(8,128)(2,1)}, u32[]{:S(2)}) copy-start(bf16[512,768]{1,0:T(8,128)(2,1)} %copy-done.79) | copy-start | bytes 2359300
  (211 other events, 1054.4 us)
Sparse Core Ops, SparseCore 0:
  14.3 29.8 all-gather.13
  76.6 26.0 reduce-scatter.12
  108.1 27.2 all-gather.15
  147.2 26.0 reduce-scatter.14
  181.1 27.2 all-gather.17
  238.7 26.0 reduce-scatter.16
  269.5 27.2 all-gather.19
  309.1 26.0 reduce-scatter.18
  344.1 27.2 all-gather.21
  402.2 26.0 reduce-scatter.20
  433.6 27.2 all-gather.23
  462.8 27.1 all-gather.35
  505.1 26.0 reduce-scatter.24
  538.0 27.2 all-gather.25
  630.4 26.0 reduce-scatter.26
  668.2 27.2 all-gather.27
  710.4 26.0 reduce-scatter.28
  742.6 27.2 all-gather.29
  834.9 26.0 reduce-scatter.30
  873.4 27.2 all-gather.31
  915.7 26.0 reduce-scatter.32
  949.2 27.2 all-gather.33
  979.2 26.0 reduce-scatter.22
  1065.7 26.1 reduce-scatter.34
  1100.8 440.7 all-reduce.4
